TPU v7x, 32 devices: a whole 2x2x4 slice. The times are simulated.
32 devices in a mesh: seq: 8 (over z, y), tensor: 2 (over x), enc: 2 (over core).
Axes of the slice: x: 2, y: 2, z: 4, core: 2. Of those that a mesh axis runs over, the one named last changes fastest.
Arguments:
- neighbour_rows: bfloat16 [8192, 1024], P('seq'), may hold values from -17 to 17
- norm_gain: float32 [1024], replicated, may hold values from 0.1 to 1.9
- up_weight: bfloat16 [1024, 4096], P(None, ('tensor', 'enc')), may hold values from -0.1875 to 0.1875
- down_weight: bfloat16 [4096, 1024], P(('tensor', 'enc')), may hold values from -0.09375 to 0.09375
- final_gain: float32 [1024], replicated, may hold values from 0.1 to 1.9
- key_weight: bfloat16 [1024, 4096], P(None, ('tensor', 'enc')), may hold values from -0.1875 to 0.1875
- value_weight: bfloat16 [1024, 4096], P(None, ('tensor', 'enc')), may hold values from -0.1875 to 0.1875
- queries: bfloat16 [8192, 4096], P('seq', ('tensor', 'enc')), may hold values from -170 to 170
- block_lists: int32 [128, 2], P('seq'), may hold values from 0 to 63, as said below
- live_counts: int32 [128], P('seq'), may hold values from 1 to 2
Outputs:
- attended: bfloat16 [8192, 4096], P('seq', ('tensor', 'enc'))
Inputs may be any that keep to these rules, and one draw needn't show every extreme that they name: `block_lists`: block b of the pool lies on the device of index b // 8 along seq. The two entries of a span name blocks of two different devices. Among all list entries of one device's spans (those beyond a span's count included) at most 4 name blocks of any one device, and in every draw some device's entries reach 4 for some device.
All inputs are finite; a program needn't handle non-finite values.
Results may differ from a plain program's by a relative error of at most 0.019.
The roundings to bfloat16 on the way count: a program that leaves them out, or rounds other values in their place, can miss the bound.
Values may be sent and summed in bfloat16 or wider, within the bound.
A program may use at most 128 MiB of HBM per device.

v0:
```python
import math

import jax
import jax.numpy as jnp
from jax import lax
from jax.sharding import PartitionSpec as P

DH = 128
NB = 128
CL = 64
KMAX = 2


def rms_scale(rows, gain):
    mean_square = jnp.mean(rows * rows, axis=-1, keepdims=True)
    return rows * lax.rsqrt(mean_square + 1e-06) * gain


def need_ranks(owners):
    need_count = owners.shape[-1]
    order_index = jnp.arange(need_count)
    same_owner = owners[..., :, None] == owners[..., None, :]
    earlier = order_index[None, :] < order_index[:, None]
    return jnp.sum(jnp.logical_and(same_owner, earlier), axis=-1)


def shards(
    neighbour_rows,
    norm_gain,
    up_weight,
    down_weight,
    final_gain,
    key_weight,
    value_weight,
    queries,
    block_lists,
    live_counts,
):
    block_rows = neighbour_rows.shape[0]
    blocks = block_rows // NB
    head_width = key_weight.shape[1]
    heads_local = head_width // DH
    row_width = 2 * head_width
    widened = neighbour_rows.astype(jnp.float32)
    normed = rms_scale(widened, norm_gain).astype(jnp.bfloat16)
    hidden = jax.nn.gelu(jnp.dot(normed, up_weight, preferred_element_type=jnp.float32)).astype(
        jnp.bfloat16
    )
    partial_sum = jnp.dot(hidden, down_weight, preferred_element_type=jnp.float32)
    encoded = widened + lax.psum(partial_sum, ("tensor", "enc"))
    final_rows = rms_scale(encoded, final_gain).astype(jnp.bfloat16)
    key_part = jnp.dot(final_rows, key_weight, preferred_element_type=jnp.float32).astype(
        jnp.bfloat16
    )
    value_part = jnp.dot(final_rows, value_weight, preferred_element_type=jnp.float32).astype(
        jnp.bfloat16
    )
    stacked = jnp.concatenate([key_part, value_part], axis=-1)
    kv_blocks = stacked.reshape(blocks, NB, row_width)
    seq_count = lax.axis_size("seq")
    span_count = live_counts.shape[0]
    need_count = span_count * KMAX
    capacity = (need_count + seq_count - 1) // seq_count
    flat_lists = block_lists.reshape(need_count)
    owners = flat_lists // blocks
    rank_order = need_ranks(owners)
    slot_index = owners * capacity + rank_order
    live_mask = jnp.arange(KMAX)[None, :] < live_counts[:, None]
    slot_range = jnp.arange(capacity)
    every_list = lax.all_gather(block_lists, "seq", axis=0, tiled=True)
    every_flat = every_list.reshape(seq_count, need_count)
    every_owner = every_flat // blocks
    every_rank = need_ranks(every_owner)
    position = lax.axis_index("seq")
    slot_match = jnp.logical_and(
        every_owner[:, :, None] == position, every_rank[:, :, None] == slot_range[None, None, :]
    )
    local_index = every_flat % blocks
    picked = jnp.sum(jnp.where(slot_match, local_index[:, :, None], 0), axis=1)
    filled = jnp.any(slot_match, axis=1)
    outgoing = jnp.take(kv_blocks, picked.reshape(-1), axis=0).reshape(
        seq_count, capacity, NB, row_width
    )
    outgoing = jnp.where(filled[:, :, None, None], outgoing, jnp.zeros((), jnp.bfloat16))
    incoming = lax.all_to_all(outgoing, "seq", split_axis=0, concat_axis=0, tiled=True)
    chosen = jnp.take(incoming.reshape(seq_count * capacity, NB, row_width), slot_index, axis=0)
    chosen = chosen.reshape(span_count, KMAX * NB, row_width)
    key_tiles = chosen[..., :head_width].reshape(span_count, KMAX * NB, heads_local, DH)
    value_tiles = chosen[..., head_width:].reshape(span_count, KMAX * NB, heads_local, DH)
    query_tiles = queries.reshape(span_count, CL, heads_local, DH)
    scores = jnp.einsum(
        "cqhd,ckhd->chqk", query_tiles, key_tiles, preferred_element_type=jnp.float32
    ) / math.sqrt(DH)
    key_mask = jnp.repeat(live_mask, NB, axis=1)
    scores = jnp.where(key_mask[:, None, None, :], scores, -1e30)
    highest = jnp.max(scores, axis=-1, keepdims=True)
    weights = jnp.exp(scores - highest)
    row_total = jnp.sum(weights, axis=-1)
    summed = jnp.einsum(
        "chqk,ckhd->cqhd",
        weights.astype(jnp.bfloat16),
        value_tiles,
        preferred_element_type=jnp.float32,
    )
    result = summed / jnp.transpose(row_total, (0, 2, 1))[..., None]
    return result.reshape(span_count * CL, head_width).astype(jnp.bfloat16)


def solution(mesh):
    placed = (
        P("seq", None),
        P(),
        P(None, ("tensor", "enc")),
        P(("tensor", "enc"), None),
        P(),
        P(None, ("tensor", "enc")),
        P(None, ("tensor", "enc")),
        P("seq", ("tensor", "enc")),
        P("seq", None),
        P("seq"),
    )
    return jax.shard_map(
        shards, mesh=mesh, in_specs=placed, out_specs=P("seq", ("tensor", "enc")), check_vma=False
    )
```

profile of v0, /device:TPU:0, one launch (start us, length us, event | category | flops | bytes accessed | tf_op | source)
XLA Modules:
  0.0 587.5 jit_solution(14996951757187758825)
XLA Ops:
  6.5 2.2 fusion.3
  8.8 8.8 %fusion.21 = f32[1024,1024]{1,0:T(8,128)} fusion(bf16[1024,1024]{1,0:T(8,128)(2,1)S(1)} %copy-done, bf16[1024,1024]{1,0:T(8,128)(2,1)} %param.12, bf16[1024,1024]{1,0:T(8,128)(2,1)} %param.10, f32[1024]{0:T(1024)} %param.11, f32[1024]{0:T(1024)S(1)} %add_rsqrt_fusion.1), kind=kOutput, calls=%fused_computation.35 | convolution fusion | flops 4308598784 | bytes 10493952 | tf_op jit(solution)/shard_map/dot_general | solution.py:49
  17.6 0.0 all-reduce.2.cloned.1.call-update
  17.7 0.6 copy-done.5
  18.3 22.4 %all-gather = s32[8,16,2]{1,2,0:T(2,128)S(1)} all-gather(s32[1,16,2]{1,2,0:T(2,128)S(1)} %bitcast.73), channel_id=1, replica_groups=mesh['seq'=8,'tensor'=2,'enc'=2] {'seq'}, dimensions={0}, use_global_device_ids=true | all-gather | bytes 1152 | tf_op jit(solution)/shard_map/all_gather | solution.py:70
  40.7 0.1 copy.75
  40.8 0.1 copy.76
  40.9 0.3 convert_reduce_fusion
  41.2 0.1 select_reduce_fusion
  41.4 0.1 copy.82
  41.4 0.1 reshape.331
  41.5 0.1 copy.81
  41.6 0.1 fusion.40
  41.8 0.1 copy.80
  41.9 64.1 %all-reduce.2.cloned.1.call-done = f32[1024,1024]{1,0:T(8,128)} async-done(((f32[1024,1024]{1,0:T(8,128)}), f32[1024,1024]{1,0:T(8,128)}) %all-reduce.2.cloned.1.call-update) | async-done | bytes 4194320 | tf_op jit(solution)/shard_map/psum | solution.py:50
  106.0 3.0 multiply_reduce_fusion
  109.0 0.5 copy-done.3
  109.4 0.7 multiply_convert_fusion
  110.2 0.8 copy-done.8
  111.0 2.4 convolution_convert_fusion
  113.5 2.4 convolution_convert_fusion.1
  115.9 2.4 pad_maximum_fusion
  118.3 6.5 %copy.92 = bf16[1024,2048]{1,0:T(8,128)(2,1)} copy(bf16[1024,2048]{0,1:T(8,128)(2,1)} %pad_maximum_fusion) | data formatting | bytes 8388608 | tf_op jit(solution)/shard_map/reshape | solution.py:59
  124.8 9.4 %gather_fusion = bf16[32,128,2048]{2,1,0:T(8,128)(2,1)} fusion(bf16[8,128,2048]{2,1,0:T(8,128)(2,1)} %bitcast.57, s32[1024]{0:T(1024)S(1)} %pad_clamp_fusion.1), kind=kCustom, calls=%fused_computation | custom fusion | bytes 33554560 | tf_op jit(solution)/shard_map/jit(_take)/gather | solution.py:81
  134.2 14.3 %select_select_fusion = bf16[8,4,128,2048]{3,2,1,0:T(8,128)(2,1)} fusion(bf16[8,4,128,2048]{3,2,1,0:T(8,128)(2,1)} %bitcast.58, pred[8,4]{1,0:T(8,128)(4,1)S(1)} %copy.81, pred[8,4]{1,0:T(8,128)(4,1)S(1)} %copy.80), kind=kLoop, calls=%fused_computation.2 | loop fusion | flops 16777216 | bytes 33554496 | tf_op jit(solution)/shard_map/jit(_where)/select_n | solution.py:84
  148.5 6.1 %all-to-all-start = ((bf16[8,4,128,2048]{3,2,1,0:T(8,128)(2,1)}), bf16[8,4,128,2048]{3,2,1,0:T(8,128)(2,1)}, u32[]{:S(2)}, u32[]{:S(2)}) async-start(bf16[8,4,128,2048]{3,2,1,0:T(8,128)(2,1)} %select_select_fusion), calls=%async_computation | async-start | bytes 33554432 | tf_op jit(solution)/shard_map/all_to_all | solution.py:85
  154.6 0.1 copy.72
  154.7 0.1 reshape.328
  154.7 0.1 reshape.333
  154.8 0.2 convert_reduce_fusion.1
  155.0 0.1 reduce_sum.59
  155.1 0.1 copy.73
  155.2 0.1 copy.74
  155.3 0.1 broadcast_in_dim.87
  155.4 0.1 iota_compare_fusion.2
  155.5 0.1 broadcast_in_dim.97
  155.6 2.2 copy.95
  157.9 359.4 %all-to-all-done = bf16[8,4,128,2048]{3,2,1,0:T(8,128)(2,1)} async-done(((bf16[8,4,128,2048]{3,2,1,0:T(8,128)(2,1)}), bf16[8,4,128,2048]{3,2,1,0:T(8,128)(2,1)}, u32[]{:S(2)}, u32[]{:S(2)}) %all-to-all-start) | async-done | bytes 16777248 | tf_op jit(solution)/shard_map/all_to_all | solution.py:85
  517.3 13.0 %gather_fusion.1 = bf16[32,128,2048]{2,1,0:T(8,128)(2,1)} fusion(bf16[32,128,2048]{2,1,0:T(8,128)(2,1)} %bitcast.5, s32[1024]{0:T(1024)S(1)} %pad_clamp_fusion), kind=kCustom, calls=%fused_computation.1 | custom fusion | bytes 33554560 | tf_op jit(solution)/shard_map/jit(_take)/gather | solution.py:86
  530.3 21.5 %copy.85 = bf16[16,256,2048]{1,2,0:T(8,128)(2,1)} copy(bf16[16,256,2048]{2,1,0:T(8,128)(2,1)} %bitcast.59) | data formatting | bytes 33554432 | tf_op jit(solution)/shard_map/jit(_take)/gather | solution.py:86
  551.9 8.8 %broadcast_select_fusion = bf16[16,256,2048]{1,2,0:T(8,128)(2,1)S(1)} fusion(bf16[16,256,2048]{1,2,0:T(8,128)(2,1)} %copy.85, pred[16,256]{1,0:T(8,128)(4,1)S(1)} %bitcast.72), kind=kLoop, calls=%fused_computation.3 | loop fusion | flops 8388608 | bytes 33558528 | tf_op jit(solution)/shard_map/jit(_take)/select_n | solution.py:86
  560.7 4.0 fusion.51
  564.6 2.2 bitcast_reduce_fusion
  566.8 3.0 fusion.1
  569.9 0.3 copy-done.4
  570.2 5.2 fusion.16
  575.4 3.4 copy.89
  578.7 1.9 copy.104
  (31 shorter events, 0.2 us)
Async XLA Ops:
  6.5 2.2 copy-start
  6.5 99.5 %all-reduce.2.cloned.1.call-start = ((), (), s32[]{:S(2)}) async-start(), calls=%async_computation.1 | async-start | bytes 8388608 | tf_op jit(solution)/shard_map/psum | solution.py:50
  17.6 0.7 copy-start.5
  17.6 88.4 %copy-start.2 = (bf16[1024,1024]{1,0:T(8,128)(2,1)S(1)}, bf16[1024,1024]{1,0:T(8,128)(2,1)}, u32[]{:S(2)}) copy-start(bf16[1024,1024]{1,0:T(8,128)(2,1)} %param.10) | copy-start | bytes 6291460
  17.6 91.3 %copy-start.6 = (f32[1024]{0:T(1024)S(1)}, f32[1024]{0:T(1024)}, u32[]{:S(2)}) copy-start(f32[1024]{0:T(1024)} %param.14) | copy-start | bytes 12292
  106.0 3.4 copy-start.3
  109.4 1.6 copy-start.8
  111.0 2.4 copy-start.9
  148.4 7.0 %copy-start.7 = (s32[16]{0:T(128)S(1)}, s32[16]{0:T(128)}, u32[]{:S(2)}) copy-start(s32[16]{0:T(128)} %param.19) | copy-start | bytes 196
  148.5 368.9 %all-to-all-start = ((bf16[8,4,128,2048]{3,2,1,0:T(8,128)(2,1)}), bf16[8,4,128,2048]{3,2,1,0:T(8,128)(2,1)}, u32[]{:S(2)}, u32[]{:S(2)}) async-start(bf16[8,4,128,2048]{3,2,1,0:T(8,128)(2,1)} %select_select_fusion), calls=%async_computation | async-start | bytes 33554432 | tf_op jit(solution)/shard_map/all_to_all | solution.py:85
  566.8 3.4 copy-start.4
  570.2 10.5 %copy-start.1 = (bf16[1024,1024]{1,0:T(8,128)(2,1)S(1)}, bf16[1024,1024]{1,0:T(8,128)(2,1)}, u32[]{:S(2)}) copy-start(bf16[1024,1024]{1,0:T(8,128)(2,1)} %param.13) | copy-start | bytes 6291460
Sparse Core Ops, SparseCore 0:
  17.8 88.1 all-reduce.1
where the time goes:
time: 589 us; the launch traced here: 588 us
  waiting for transfers between devices  424 us (72%)
  local copies, waits for them, and re-layouts  65.5 us (11%)
  other arithmetic  35.3 us (6%)
  blocking collectives  22.4 us (4%)
  matrix products  21 us (4%)
  between operations  13.6 us (2%)
  starting transfers between devices  6.11 us (1%)
    all_to_all x1, waiting for transfers between devices, shards(): lax.all_to_all(outgoing, 'seq', split_axis=0, concat_axis=0, tiled=True)  359 us
    psum x1, waiting for transfers between devices, shards(): encoded = widened + lax.psum(partial_sum, ('tensor', 'enc'))  64.1 us
    gather x2, local copies, waits for them, and re-layouts, shards(): jnp.take(incoming.reshape(seq_count * capacity, NB, row_width), slot_inde...  34.6 us
    all_gather x1, blocking collectives, shards(): every_list = lax.all_gather(block_lists, 'seq', axis=0, tiled=True)  22.4 us
    select_n x1, other arithmetic, shards(): jnp.where(filled[:, :, None, None], outgoing, jnp.zeros((), jnp.bfloat16))  14.3 us
  transfers between devices with their start and end apart: 2, of which 2 were waited for; matrix products, arithmetic and copies ran while one was open for 1% of the time, Pallas kernels for 0%

commit v1 on v0

v1 whole, which is shorter than its diff:
```python
import functools
import math

import jax
import jax.numpy as jnp
from jax import lax
from jax.experimental import pallas as pl
from jax.experimental.pallas import tpu as pltpu
from jax.sharding import PartitionSpec as P

DH = 128
NB = 128
CL = 64
KMAX = 2
GROUP = ("tensor", "enc")


def rms_scale(rows, gain):
    mean_square = jnp.mean(rows * rows, axis=-1, keepdims=True)
    return rows * lax.rsqrt(mean_square + 1e-06) * gain


def need_ranks(owners):
    need_count = owners.shape[-1]
    order_index = jnp.arange(need_count)
    same_owner = owners[..., :, None] == owners[..., None, :]
    earlier = order_index[None, :] < order_index[:, None]
    return jnp.sum(jnp.logical_and(same_owner, earlier), axis=-1)


def attend_kernel(heads, slots, live, q_ref, k0_ref, k1_ref, v0_ref, v1_ref, o_ref):
    span = pl.program_id(0)
    both = live[span] > 1
    width = heads * DH
    k0 = k0_ref[...].reshape(NB, width)
    k1 = k1_ref[...].reshape(NB, width)
    v0 = v0_ref[...].reshape(NB, width)
    v1 = v1_ref[...].reshape(NB, width)
    contract = (((1,), (1,)), ((), ()))
    for head in range(heads):
        cols = slice(head * DH, (head + 1) * DH)
        q = q_ref[:, cols]
        s0 = lax.dot_general(q, k0[:, cols], contract, preferred_element_type=jnp.float32)
        s1 = lax.dot_general(q, k1[:, cols], contract, preferred_element_type=jnp.float32)
        s0 = s0 / math.sqrt(DH)
        s1 = jnp.where(both, s1 / math.sqrt(DH), -1e30)
        highest = jnp.max(jnp.maximum(s0, s1), axis=-1, keepdims=True)
        w0 = jnp.exp(s0 - highest)
        w1 = jnp.exp(s1 - highest)
        total = jnp.sum(w0 + w1, axis=-1, keepdims=True)
        summed = jnp.dot(
            w0.astype(jnp.bfloat16), v0[:, cols], preferred_element_type=jnp.float32
        ) + jnp.dot(w1.astype(jnp.bfloat16), v1[:, cols], preferred_element_type=jnp.float32)
        o_ref[:, cols] = (summed / total).astype(o_ref.dtype)


def attend(queries, keys, values, slots, live):
    parts, _, rows, width = keys.shape
    spans = live.shape[0]

    def block(entry):
        return pl.BlockSpec(
            (parts, 1, rows, width), lambda c, slots, live: (0, slots[c * KMAX + entry], 0, 0)
        )

    rows_of = pl.BlockSpec((CL, width), lambda c, slots, live: (c, 0))
    return pl.pallas_call(
        functools.partial(attend_kernel, width // DH),
        out_shape=jax.ShapeDtypeStruct(queries.shape, jnp.bfloat16),
        grid_spec=pltpu.PrefetchScalarGridSpec(
            num_scalar_prefetch=2,
            grid=(spans,),
            in_specs=[rows_of, block(0), block(1), block(0), block(1)],
            out_specs=rows_of,
        ),
        compiler_params=pltpu.CompilerParams(vmem_limit_bytes=32 * 2**20),
    )(slots, live, queries, keys, keys, values, values)


def shards(
    neighbour_rows,
    norm_gain,
    up_weight,
    down_weight,
    final_gain,
    key_weight,
    value_weight,
    queries,
    block_lists,
    live_counts,
):
    features = neighbour_rows.shape[1]
    blocks = neighbour_rows.shape[0] // NB
    group = lax.axis_size("tensor") * lax.axis_size("enc")
    part = NB // group
    seq_count = lax.axis_size("seq")
    span_count = live_counts.shape[0]
    need_count = span_count * KMAX
    capacity = (need_count + seq_count - 1) // seq_count

    flat_lists = block_lists.reshape(need_count)
    owners = flat_lists // blocks
    slot_index = owners * capacity + need_ranks(owners)
    every_list = lax.all_gather(block_lists, "seq", axis=0, tiled=True)
    every_flat = every_list.reshape(seq_count, need_count)
    every_owner = every_flat // blocks
    every_rank = need_ranks(every_owner)
    position = lax.axis_index("seq")
    slot_match = jnp.logical_and(
        every_owner[:, :, None] == position,
        every_rank[:, :, None] == jnp.arange(capacity)[None, None, :],
    )
    local_index = every_flat % blocks
    picked = jnp.sum(jnp.where(slot_match, local_index[:, :, None], 0), axis=1).reshape(-1)
    chosen = (picked[:, None] == jnp.arange(blocks)[None, :]).astype(jnp.bfloat16)

    spread = jnp.transpose(neighbour_rows.reshape(blocks, group, part, features), (1, 0, 2, 3))
    widened = spread.reshape(group * blocks * part, features).astype(jnp.float32)
    normed = rms_scale(widened, norm_gain).astype(jnp.bfloat16)
    hidden = jax.nn.gelu(jnp.dot(normed, up_weight, preferred_element_type=jnp.float32)).astype(
        jnp.bfloat16
    )
    partial_sum = jnp.dot(hidden, down_weight, preferred_element_type=jnp.float32)
    summed = lax.psum_scatter(partial_sum, GROUP, scatter_dimension=0, tiled=True)
    me = lax.axis_index("tensor") * lax.axis_size("enc") + lax.axis_index("enc")
    own = lax.dynamic_index_in_dim(spread, me, 0, keepdims=False)
    encoded = own.reshape(blocks * part, features).astype(jnp.float32) + summed
    final_rows = rms_scale(encoded, final_gain).astype(jnp.bfloat16)
    outgoing = jnp.dot(
        chosen,
        final_rows.reshape(blocks, part * features),
        preferred_element_type=jnp.float32,
    ).astype(jnp.bfloat16)
    outgoing = outgoing.reshape(seq_count, capacity * part, features)
    incoming = lax.all_to_all(outgoing, "seq", split_axis=0, concat_axis=0, tiled=True)
    gathered = lax.all_gather(incoming, GROUP, axis=0, tiled=True)
    gathered = gathered.reshape(-1, features)
    shape = (group, seq_count * capacity, part, key_weight.shape[1])
    keys = jnp.dot(gathered, key_weight, preferred_element_type=jnp.float32).astype(jnp.bfloat16)
    values = jnp.dot(gathered, value_weight, preferred_element_type=jnp.float32).astype(
        jnp.bfloat16
    )
    return attend(queries, keys.reshape(shape), values.reshape(shape), slot_index, live_counts)


def solution(mesh):
    placed = (
        P("seq", None),
        P(),
        P(None, GROUP),
        P(GROUP, None),
        P(),
        P(None, GROUP),
        P(None, GROUP),
        P("seq", GROUP),
        P("seq", None),
        P("seq"),
    )
    return jax.shard_map(
        shards, mesh=mesh, in_specs=placed, out_specs=P("seq", GROUP), check_vma=False
    )
```

time: 589 us -> 260 us (0.44)
  waiting for transfers between devices: 424 us -> 78.7 us
  local copies, waits for them, and re-layouts: 65.5 us -> 9.24 us
  blocking collectives: 22.4 us -> 76.1 us
  Pallas kernels: 0 us -> 37.9 us
  other arithmetic: 35.3 us -> 9.91 us
  matrix products: 21 us -> 34.3 us
  starting transfers between devices: 6.11 us -> 0.04 us
    all_to_all x1 -> x0, waiting for transfers between devices: 359 us -> none  [shards(): lax.all_to_all(outgoing, 'seq', split_axis=0, concat_axis=0, tiled=True)]
    psum x1 -> x0, waiting for transfers between devices: 64.1 us -> none  [shards(): encoded = widened + lax.psum(partial_sum, ('tensor', 'enc'))]
    all_gather x0 -> x1, waiting for transfers between devices: none -> 56.1 us  [shards(): gathered = lax.all_gather(incoming, GROUP, axis=0, tiled=True)]
    all_to_all x0 -> x1, blocking collectives: none -> 53.9 us  [shards(): lax.all_to_all(outgoing, 'seq', split_axis=0, concat_axis=0, tiled=True)]
    gather x3 -> x0, local copies, waits for them, and re-layouts: 44 us -> none  [the longest x2 34.6 us: shards(): jnp.take(incoming.reshape(seq_count * capacity, NB, row_width), slot_inde...]
    pallas_call x0 -> x1, Pallas kernels: none -> 37.9 us  [attend(): pl.pallas_call(functools.partial(attend_kernel, width // DH), out_shape=j...]
    select_n x4 -> x0, other arithmetic: 23.1 us -> none  [the longest x1 14.3 us: shards(): jnp.where(filled[:, :, None, None], outgoing, jnp.zeros((), jnp.bfloat16))]
    reduce_scatter x0 -> x1, waiting for transfers between devices: none -> 22.5 us  [shards(): lax.psum_scatter(partial_sum, GROUP, scatter_dimension=0, tiled=True)]
where the time goes in v1:
time: 260 us
  waiting for transfers between devices  78.7 us (30%)
  blocking collectives  76.1 us (29%)
  Pallas kernels  37.9 us (15%)
  matrix products  34.3 us (13%)
  between operations  13.6 us (5%)
  other arithmetic  9.91 us (4%)
  local copies, waits for them, and re-layouts  9.24 us (4%)
    all_gather x1, waiting for transfers between devices, shards(): gathered = lax.all_gather(incoming, GROUP, axis=0, tiled=True)  56.1 us
    all_to_all x1, blocking collectives, shards(): lax.all_to_all(outgoing, 'seq', split_axis=0, concat_axis=0, tiled=True)  53.9 us
    pallas_call x1, Pallas kernels, attend(): pl.pallas_call(functools.partial(attend_kernel, width // DH), out_shape=j...  37.9 us
    reduce_scatter x1, waiting for transfers between devices, shards(): lax.psum_scatter(partial_sum, GROUP, scatter_dimension=0, tiled=True)  22.5 us
    all_gather x1, blocking collectives, shards(): every_list = lax.all_gather(block_lists, 'seq', axis=0, tiled=True)  22.3 us
    dot_general x1, matrix products, shards(): jnp.dot(gathered, value_weight, preferred_element_type=jnp.float32)  11.4 us
    dot_general x1, matrix products, shards(): jnp.dot(gathered, key_weight, preferred_element_type=jnp.float32)  11.4 us
    dot_general x1, matrix products, shards(): jnp.dot(hidden, down_weight, preferred_element_type=jnp.float32)  9.36 us
  transfers between devices with their start and end apart: 2, of which 2 were waited for; matrix products, arithmetic and copies ran while one was open for 1% of the time, Pallas kernels for 0%

profile of v1, /device:TPU:0, one launch (start us, length us, event | category | flops | bytes accessed | tf_op | source)
XLA Modules:
  0.0 259.8 jit_solution(5042316844352979681)
XLA Ops:
  6.5 0.0 copy-start
  6.5 0.0 reduce-scatter.2.cloned.1.call-start
  6.5 0.0 copy-start.3
  6.5 4.2 %convert_bitcast_fusion = f32[4,8,32,1024]{3,2,0,1:T(8,128)} fusion(bf16[1024,1024]{1,0:T(8,128)(2,1)} %param.10), kind=kLoop, calls=%fused_computation.5 | loop fusion | flops 1048576 | bytes 6291456 | tf_op jit(solution)/shard_map/convert_element_type | solution.py:118
  10.7 0.0 copy-done.3
  10.7 0.5 fusion
  11.2 0.1 rsqrt.20
  11.3 0.0 copy-start.4
  11.3 2.5 copy.50
  13.8 0.0 copy-done.4
  13.8 1.7 fusion.10
  15.5 9.4 %fusion.11 = f32[1024,1024]{1,0:T(8,128)} fusion(bf16[1024,1024]{1,0:T(8,128)(2,1)} %param.13, bf16[1024,1024]{1,0:T(8,128)(2,1)} %fusion.10, bf16[1024,1024]{1,0:T(8,128)(2,1)} %param.12), kind=kOutput, calls=%fused_computation.18 | convolution fusion | flops 4304404480 | bytes 10485760 | tf_op jit(solution)/shard_map/dot_general | solution.py:123
  24.9 0.0 copy-start.6
  24.9 0.0 copy-start.5
  24.9 0.0 reduce-scatter.2.cloned.1.call-update
  24.9 0.0 all-gather.3.cloned.1.call-start
  25.0 0.6 copy-done.6
  25.6 22.3 %all-gather = s32[8,16,2]{1,2,0:T(2,128)S(1)} all-gather(s32[1,16,2]{1,2,0:T(2,128)S(1)} %bitcast.36), channel_id=1, replica_groups=mesh['seq'=8,'tensor'=2,'enc'=2] {'seq'}, dimensions={0}, use_global_device_ids=true | all-gather | bytes 1152 | tf_op jit(solution)/shard_map/all_gather | solution.py:104
  47.8 0.1 copy.44
  47.9 0.1 copy.45
  48.0 0.3 convert_reduce_fusion
  48.3 0.1 select_reduce_fusion
  48.5 0.1 copy.49
  48.6 0.1 eq.78
  48.6 1.1 constant_dynamic-slice_fusion
  49.7 22.5 %reduce-scatter.2.cloned.1.call-done = f32[256,1024]{1,0:T(8,128)} async-done(((f32[1024,1024]{1,0:T(8,128)}), f32[256,1024]{1,0:T(8,128)}) %reduce-scatter.2.cloned.1.call-update) | async-done | bytes 1048592 | tf_op jit(solution)/shard_map/reduce_scatter | solution.py:124
  72.3 1.4 multiply_reduce_fusion
  73.7 0.0 copy-done.5
  73.7 1.4 multiply_convert_fusion
  75.1 0.2 reshape.221
  75.4 2.1 convolution_convert_fusion
  77.5 4.2 %reshape.222 = bf16[8,128,1024]{2,1,0:T(8,128)(2,1)} reshape(bf16[32,32768]{1,0:T(8,128)(2,1)} %convolution_convert_fusion) | data formatting | bytes 4194304 | tf_op jit(solution)/shard_map/reshape | solution.py:134
  81.7 53.9 %all_to_all.5 = bf16[8,128,1024]{2,1,0:T(8,128)(2,1)} all-to-all(bf16[8,128,1024]{2,1,0:T(8,128)(2,1)} %reshape.222), channel_id=1, replica_groups=mesh['seq'=8,'tensor'=2,'enc'=2] {'seq'}, dimensions={0} | all-to-all | bytes 4194304 | tf_op jit(solution)/shard_map/all_to_all | solution.py:135
  135.5 0.0 all-gather.3.cloned.1.call-update
  135.5 0.1 copy.43
  135.6 0.1 reshape.218
  135.7 0.2 convert_reduce_fusion.1
  135.9 56.1 %all-gather.3.cloned.1.call-done = bf16[32,128,1024]{2,1,0:T(8,128)(2,1)} async-done(((bf16[8,128,1024]{2,1,0:T(8,128)(2,1)}), bf16[32,128,1024]{2,1,0:T(8,128)(2,1)}) %all-gather.3.cloned.1.call-update) | async-done | bytes 8388624 | tf_op jit(solution)/shard_map/all_gather | solution.py:136
  192.1 0.0 copy-done
  192.1 0.0 copy-start.7
  192.1 11.4 %convolution_convert_fusion.2 = bf16[4096,1024]{1,0:T(8,128)(2,1)S(1)} fusion(bf16[4096,1024]{1,0:T(8,128)(2,1)} %bitcast.37, bf16[1024,1024]{1,0:T(8,128)(2,1)S(1)} %copy-done), kind=kOutput, calls=%fused_computation.2 | convolution fusion | flops 8594128896 | bytes 18874368 | tf_op jit(solution)/shard_map/dot_general | solution.py:139
  203.5 0.0 copy-done.7
  203.5 0.0 copy-start.1
  203.5 0.0 copy-start.2
  203.5 11.4 %convolution_convert_fusion.1 = bf16[4096,1024]{1,0:T(8,128)(2,1)S(1)} fusion(bf16[4096,1024]{1,0:T(8,128)(2,1)} %bitcast.38, bf16[1024,1024]{1,0:T(8,128)(2,1)S(1)} %copy-done.7), kind=kOutput, calls=%fused_computation.1 | convolution fusion | flops 8594128896 | bytes 18874368 | tf_op jit(solution)/shard_map/dot_general | solution.py:140
  215.0 0.0 copy-done.1
  215.0 0.0 copy-done.2
  215.0 37.9 %shard_map.100 = bf16[1024,1024]{1,0:T(8,128)(2,1)} custom-call(s32[32]{0:T(128)S(1)} %multiply_add_fusion.slots, s32[16]{0:T(128)S(1)} %copy-done.2, bf16[1024,1024]{1,0:T(8,128)(2,1)S(1)} %copy-done.1, bf16[4,32,32,1024]{3,2,1,0:T(8,128)(2,1)S(1)} %bitcast.29, bf16[4,32,32,1024]{3,2,1,0:T(8,128)(2,1)S(1)} %bitcast.30, ...), custom_call_target="tpu_custom_call" | custom-call | tf_op jit(solution)/shard_map/pallas_call | solution.py:67
  (8 shorter events, 0.1 us)
Async XLA Ops:
  6.5 185.5 %copy-start = (bf16[1024,1024]{1,0:T(8,128)(2,1)S(1)}, bf16[1024,1024]{1,0:T(8,128)(2,1)}, u32[]{:S(2)}) copy-start(bf16[1024,1024]{1,0:T(8,128)(2,1)} %param.15) | copy-start | bytes 6291460
  6.5 65.7 %reduce-scatter.2.cloned.1.call-start = ((), (), s32[]{:S(2)}) async-start(), calls=%async_computation.2 | async-start | bytes 5242880 | tf_op jit(solution)/shard_map/reduce_scatter | solution.py:124
  6.5 4.2 %copy-start.3 = (bf16[1024,1024]{1,0:T(8,128)(2,1)S(1)}, bf16[1024,1024]{1,0:T(8,128)(2,1)}, u32[]{:S(2)}) copy-start(bf16[1024,1024]{1,0:T(8,128)(2,1)} %param.10) | copy-start | bytes 6291460
  11.3 2.5 copy-start.4
  24.9 0.7 copy-start.6
  24.9 48.8 %copy-start.5 = (f32[1024]{0:T(1024)S(1)}, f32[1024]{0:T(1024)}, u32[]{:S(2)}) copy-start(f32[1024]{0:T(1024)} %param.14) | copy-start | bytes 12292
  24.9 167.1 %all-gather.3.cloned.1.call-start = ((), (), s32[]{:S(2)}) async-start(), calls=%async_computation.3 | async-start | bytes 10485760 | tf_op jit(solution)/shard_map/all_gather | solution.py:136
  192.1 11.4 %copy-start.7 = (bf16[1024,1024]{1,0:T(8,128)(2,1)S(1)}, bf16[1024,1024]{1,0:T(8,128)(2,1)}, u32[]{:S(2)}) copy-start(bf16[1024,1024]{1,0:T(8,128)(2,1)} %param.16) | copy-start | bytes 6291460
  203.5 11.5 %copy-start.1 = (bf16[1024,1024]{1,0:T(8,128)(2,1)S(1)}, bf16[1024,1024]{1,0:T(8,128)(2,1)}, u32[]{:S(2)}) copy-start(bf16[1024,1024]{1,0:T(8,128)(2,1)} %q_ref.1) | copy-start | bytes 6291460
  203.5 11.5 %copy-start.2 = (s32[16]{0:T(128)S(1)}, s32[16]{0:T(128)}, u32[]{:S(2)}) copy-start(s32[16]{0:T(128)} %live.1) | copy-start | bytes 196
Sparse Core Ops, SparseCore 0:
  25.0 47.1 reduce-scatter.1
  135.7 56.3 all-gather.2

commit v2 on v1

--- a/solution.py
+++ b/solution.py
@@ -30,38 +30,42 @@
 
 def attend_kernel(heads, slots, live, q_ref, k0_ref, k1_ref, v0_ref, v1_ref, o_ref):
     span = pl.program_id(0)
-    both = live[span] > 1
     width = heads * DH
     k0 = k0_ref[...].reshape(NB, width)
     k1 = k1_ref[...].reshape(NB, width)
     v0 = v0_ref[...].reshape(NB, width)
     v1 = v1_ref[...].reshape(NB, width)
     contract = (((1,), (1,)), ((), ()))
-    for head in range(heads):
-        cols = slice(head * DH, (head + 1) * DH)
-        q = q_ref[:, cols]
-        s0 = lax.dot_general(q, k0[:, cols], contract, preferred_element_type=jnp.float32)
-        s1 = lax.dot_general(q, k1[:, cols], contract, preferred_element_type=jnp.float32)
-        s0 = s0 / math.sqrt(DH)
-        s1 = jnp.where(both, s1 / math.sqrt(DH), -1e30)
-        highest = jnp.max(jnp.maximum(s0, s1), axis=-1, keepdims=True)
-        w0 = jnp.exp(s0 - highest)
-        w1 = jnp.exp(s1 - highest)
-        total = jnp.sum(w0 + w1, axis=-1, keepdims=True)
-        summed = jnp.dot(
-            w0.astype(jnp.bfloat16), v0[:, cols], preferred_element_type=jnp.float32
-        ) + jnp.dot(w1.astype(jnp.bfloat16), v1[:, cols], preferred_element_type=jnp.float32)
-        o_ref[:, cols] = (summed / total).astype(o_ref.dtype)
-
-
-def attend(queries, keys, values, slots, live):
-    parts, _, rows, width = keys.shape
+    columns = [slice(head * DH, (head + 1) * DH) for head in range(heads)]
+    keys = jnp.concatenate([k0, k1], axis=0)
+    values = jnp.concatenate([v0, v1], axis=0)
+    place = lax.broadcasted_iota(jnp.int32, (CL, KMAX * NB), 1)
+    kept = place < live[span] * NB
+    scores = [
+        lax.dot_general(q_ref[:, c], keys[:, c], contract, preferred_element_type=jnp.float32)
+        for c in columns
+    ]
+    scores = [jnp.where(kept, s / math.sqrt(DH), -1e30) for s in scores]
+    weights = [jnp.exp(s - jnp.max(s, axis=-1, keepdims=True)) for s in scores]
+    totals = [jnp.sum(w, axis=-1, keepdims=True) for w in weights]
+    sums = [
+        jnp.dot(w.astype(jnp.bfloat16), values[:, c], preferred_element_type=jnp.float32)
+        for w, c in zip(weights, columns)
+    ]
+    for c, summed, total in zip(columns, sums, totals):
+        o_ref[:, c] = (summed / total).astype(o_ref.dtype)
+
+
+def attend(queries, keys, values, slots, live, capacity):
+    chunks, _, parts, _, rows, width = keys.shape
     spans = live.shape[0]
 
     def block(entry):
-        return pl.BlockSpec(
-            (parts, 1, rows, width), lambda c, slots, live: (0, slots[c * KMAX + entry], 0, 0)
-        )
+        def place(c, slots, live):
+            slot = slots[c * KMAX + entry]
+            return (0, slot // capacity, 0, lax.rem(slot, capacity), 0, 0)
+
+        return pl.BlockSpec((chunks, 1, parts, 1, rows, width), place)
 
     rows_of = pl.BlockSpec((CL, width), lambda c, slots, live: (c, 0))
     return pl.pallas_call(
@@ -75,6 +79,360 @@
         ),
         compiler_params=pltpu.CompilerParams(vmem_limit_bytes=32 * 2**20),
     )(slots, live, queries, keys, keys, values, values)
+
+
+MESH = pl.DeviceIdType.MESH
+TILE = 256
+CHUNKS = 2
+
+
+def exchange_kernel(
+    capacity,
+    rows_ref,
+    gain_ref,
+    up_ref,
+    down_ref,
+    final_ref,
+    key_ref,
+    value_ref,
+    want_ref,
+    keys_ref,
+    values_ref,
+    normed,
+    hidden,
+    sums,
+    core_sums,
+    far_sums,
+    finals,
+    wanted,
+    outgoing,
+    landed,
+    key_stage,
+    value_stage,
+    list_send,
+    list_recv,
+    sum_send,
+    sum_recv,
+    far_send,
+    far_recv,
+    pick_send,
+    pick_recv,
+    x_send,
+    x_recv,
+    core_send,
+    core_recv,
+    diag_send,
+    diag_recv,
+    key_sem,
+    value_sem,
+):
+    seq_count = want_ref.shape[0]
+    features = rows_ref.shape[-1]
+    chunk_rows = finals.shape[1]
+    piece = outgoing.shape[1] // capacity
+    tile_rows = 4 * outgoing.shape[1]
+    steps = CHUNKS * seq_count
+    seq, ten, enc = lax.axis_index("seq"), lax.axis_index("tensor"), lax.axis_index("enc")
+    x_mate = (seq, 1 - ten, enc)
+    core_mate = (seq, ten, 1 - enc)
+
+    def peer(offset):
+        return (lax.rem(seq + offset + seq_count, seq_count), ten, enc)
+
+    barrier = pltpu.get_barrier_semaphore()
+    for offset in range(1, seq_count):
+        pl.semaphore_signal(barrier, inc=1, device_id=peer(offset), device_id_type=MESH)
+    for mate in (x_mate, core_mate):
+        pl.semaphore_signal(barrier, inc=1, device_id=mate, device_id_type=MESH)
+    pl.semaphore_wait(barrier, seq_count + 1)
+
+    def remote(src, dst, send, recv, device):
+        return pltpu.make_async_remote_copy(
+            src_ref=src,
+            dst_ref=dst,
+            send_sem=send,
+            recv_sem=recv,
+            device_id=device,
+            device_id_type=MESH,
+        )
+
+    def list_copy(k):
+        return remote(
+            want_ref.at[k], wanted.at[k], list_send.at[k], list_recv.at[k], peer(-k)
+        )
+
+    for k in range(1, seq_count):
+        list_copy(k).start()
+
+    def feed_forward(order, member):
+        rows = rows_ref[member].astype(jnp.float32)
+        normed[...] = rms_scale(rows, gain_ref[...]).astype(jnp.bfloat16)
+
+        @pl.loop(0, up_ref.shape[1] // TILE)
+        def _(n):
+            cols = pl.ds(pl.multiple_of(n * TILE, TILE), TILE)
+            hidden[:, cols] = jax.nn.gelu(
+                jnp.dot(normed[...], up_ref[:, cols], preferred_element_type=jnp.float32)
+            ).astype(jnp.bfloat16)
+
+        @pl.loop(0, features // TILE)
+        def _(n):
+            cols = pl.ds(pl.multiple_of(n * TILE, TILE), TILE)
+            sums[order, :, cols] = jnp.dot(
+                hidden[...], down_ref[:, cols], preferred_element_type=jnp.float32
+            )
+
+    def sum_copy(i):
+        return remote(
+            sums.at[2 * i], core_sums.at[i], sum_send.at[i], sum_recv.at[i], core_mate
+        )
+
+    def far_copy(c):
+        span = pl.ds(c * chunk_rows, chunk_rows)
+        return remote(
+            sums.at[1, span], far_sums.at[c], far_send.at[c], far_recv.at[c], x_mate
+        )
+
+    feed_forward(0, 2 * (1 - ten) + 1 - enc)
+    sum_copy(0).start()
+    feed_forward(1, 2 * (1 - ten) + enc)
+    sum_copy(0).wait_recv()
+    for c in range(CHUNKS):
+        span = pl.ds(c * chunk_rows, chunk_rows)
+        sums[1, span, :] += core_sums[0, span, :]
+        far_copy(c).start()
+    feed_forward(2, 2 * ten + 1 - enc)
+    sum_copy(1).start()
+    feed_forward(3, 2 * ten + enc)
+    sum_copy(1).wait_recv()
+
+    def pick_copy(s, k):
+        return remote(
+            outgoing.at[s], landed.at[0, s], pick_send.at[s], pick_recv.at[s], peer(k)
+        )
+
+    lane = lax.broadcasted_iota(jnp.int32, (piece, chunk_rows), 1)
+    row = lax.broadcasted_iota(jnp.int32, (piece, chunk_rows), 0)
+    same_row = lax.rem(lane, piece) == row
+    lane_block = lax.div(lane, piece)
+
+    def pick(c, want):
+        marks = [
+            jnp.where(
+                jnp.logical_and(want[t : t + 1, :] == lane_block, same_row), 1.0, 0.0
+            ).astype(jnp.bfloat16)
+            for t in range(capacity)
+        ]
+        return jnp.dot(
+            jnp.concatenate(marks, axis=0), finals[c], preferred_element_type=jnp.float32
+        ).astype(jnp.bfloat16)
+
+    for c in range(CHUNKS):
+        span = pl.ds(c * chunk_rows, chunk_rows)
+        far_copy(c).wait_recv()
+        encoded = rows_ref[2 * ten + enc, span, :].astype(jnp.float32) + (
+            (sums[3, span, :] + core_sums[1, span, :]) + far_sums[c]
+        )
+        finals[c] = rms_scale(encoded, final_ref[...]).astype(jnp.bfloat16)
+        landed[0, c * seq_count] = pick(c, want_ref[0])
+
+        @pl.loop(1, seq_count)
+        def _(k):
+            if c == 0:
+                list_copy(k).wait_recv()
+            outgoing[c * seq_count + k] = pick(c, wanted[k])
+            pick_copy(c * seq_count + k, k).start()
+
+    def x_copy(s):
+        return remote(landed.at[0, s], landed.at[1, s], x_send.at[s], x_recv.at[s], x_mate)
+
+    def core_copy(s):
+        return remote(
+            landed.at[0, s], landed.at[2, s], core_send.at[s], core_recv.at[s], core_mate
+        )
+
+    def diag_copy(s):
+        return remote(
+            landed.at[1, s], landed.at[3, s], diag_send.at[s], diag_recv.at[s], core_mate
+        )
+
+    def store_copies(s):
+        slot = lax.rem(s, 2)
+        return (
+            pltpu.make_async_copy(key_stage.at[slot], keys_ref.at[s], key_sem.at[slot]),
+            pltpu.make_async_copy(value_stage.at[slot], values_ref.at[s], value_sem.at[slot]),
+        )
+
+    @pl.loop(0, steps + 2)
+    def _(s):
+        @pl.when(s < steps)
+        def _():
+            k = lax.rem(s, seq_count)
+
+            @pl.when(k > 0)
+            def _():
+                pick_copy(s, k).wait_recv()
+
+            x_copy(s).start()
+            core_copy(s).start()
+
+        @pl.when(jnp.logical_and(s >= 1, s < steps + 1))
+        def _():
+            x_copy(s - 1).wait_recv()
+            diag_copy(s - 1).start()
+
+        @pl.when(s >= 2)
+        def _():
+            done = s - 2
+            core_copy(done).wait_recv()
+            diag_copy(done).wait_recv()
+
+            @pl.when(done >= 2)
+            def _():
+                for copy in store_copies(done - 2):
+                    copy.wait()
+
+            slot = lax.rem(done, 2)
+            rows = landed[:, done].reshape(tile_rows, features)
+
+            @pl.loop(0, key_ref.shape[1] // TILE)
+            def _(n):
+                cols = pl.ds(pl.multiple_of(n * TILE, TILE), TILE)
+                key_stage[slot, :, cols] = jnp.dot(
+                    rows, key_ref[:, cols], preferred_element_type=jnp.float32
+                ).astype(jnp.bfloat16)
+                value_stage[slot, :, cols] = jnp.dot(
+                    rows, value_ref[:, cols], preferred_element_type=jnp.float32
+                ).astype(jnp.bfloat16)
+
+            for copy in store_copies(done):
+                copy.start()
+
+    for s in (steps - 2, steps - 1):
+        for copy in store_copies(s):
+            copy.wait()
+    for k in range(1, seq_count):
+        list_copy(k).wait_send()
+    for i in range(2):
+        sum_copy(i).wait_send()
+    for c in range(CHUNKS):
+        far_copy(c).wait_send()
+
+    @pl.loop(0, steps)
+    def _(s):
+        @pl.when(lax.rem(s, seq_count) > 0)
+        def _():
+            pick_copy(s, lax.rem(s, seq_count)).wait_send()
+
+        x_copy(s).wait_send()
+        core_copy(s).wait_send()
+        diag_copy(s).wait_send()
+
+
+def exchange(rows, norm_gain, up, down, final_gain, key_weight, value_weight, want, capacity):
+    group, part_rows, features = rows.shape
+    seq_count = want.shape[0]
+    steps = CHUNKS * seq_count
+    width = key_weight.shape[1]
+    chunk_rows = part_rows // CHUNKS
+    piece_rows = capacity * (NB // group // CHUNKS)
+    out = jax.ShapeDtypeStruct((steps, group * piece_rows, width), jnp.bfloat16)
+    bf16, f32 = jnp.bfloat16, jnp.float32
+    dma = pltpu.SemaphoreType.DMA
+    rows_out = 2 * group * piece_rows * seq_count * CHUNKS * features * width
+    return pl.pallas_call(
+        functools.partial(exchange_kernel, capacity),
+        out_shape=(out, out),
+        in_specs=[pl.BlockSpec(memory_space=pltpu.VMEM)] * 8,
+        out_specs=(pl.BlockSpec(memory_space=pl.ANY),) * 2,
+        scratch_shapes=[
+            pltpu.VMEM((part_rows, features), bf16),
+            pltpu.VMEM((part_rows, up.shape[1]), bf16),
+            pltpu.VMEM((group, part_rows, features), f32),
+            pltpu.VMEM((2, part_rows, features), f32),
+            pltpu.VMEM((CHUNKS, chunk_rows, features), f32),
+            pltpu.VMEM((CHUNKS, chunk_rows, features), bf16),
+            pltpu.VMEM(want.shape, jnp.int32),
+            pltpu.VMEM((steps, piece_rows, features), bf16),
+            pltpu.VMEM((group, steps, piece_rows, features), bf16),
+            pltpu.VMEM((2, group * piece_rows, width), bf16),
+            pltpu.VMEM((2, group * piece_rows, width), bf16),
+            dma((seq_count,)),
+            dma((seq_count,)),
+            dma((2,)),
+            dma((2,)),
+            dma((CHUNKS,)),
+            dma((CHUNKS,)),
+            *[dma((steps,)) for _ in range(8)],
+            dma((2,)),
+            dma((2,)),
+        ],
+        compiler_params=pltpu.CompilerParams(
+            collective_id=0, has_side_effects=True, vmem_limit_bytes=56 * 2**20
+        ),
+        cost_estimate=pl.CostEstimate(
+            flops=2 * rows_out, bytes_accessed=32 * 2**20, transcendentals=0
+        ),
+    )(
+        rows,
+        norm_gain.reshape(1, -1),
+        up,
+        down,
+        final_gain.reshape(1, -1),
+        key_weight,
+        value_weight,
+        want,
+    )
+
+
+def exchanged_attention(
+    neighbour_rows,
+    norm_gain,
+    up_weight,
+    down_weight,
+    final_gain,
+    key_weight,
+    value_weight,
+    queries,
+    block_lists,
+    live_counts,
+):
+    features = neighbour_rows.shape[1]
+    blocks = neighbour_rows.shape[0] // NB
+    group = lax.axis_size("tensor") * lax.axis_size("enc")
+    piece = NB // group // CHUNKS
+    seq_count = lax.axis_size("seq")
+    need_count = live_counts.shape[0] * KMAX
+    capacity = (need_count + seq_count - 1) // seq_count
+    width = key_weight.shape[1]
+    flat_lists = block_lists.reshape(need_count)
+    behind = lax.rem(lax.axis_index("seq") - flat_lists // blocks + seq_count, seq_count)
+    slot_index = behind * capacity + need_ranks(behind)
+    places = jnp.arange(seq_count * capacity)
+    chosen = slot_index[None, :] == places[:, None]
+    picked = jnp.sum(jnp.where(chosen, (flat_lists % blocks)[None, :], 0), axis=1)
+    want = jnp.broadcast_to(
+        picked.reshape(seq_count, capacity, 1), (seq_count, capacity, blocks * piece)
+    )
+    want = jnp.pad(want, ((0, 0), (0, -capacity % 8), (0, 0))).astype(jnp.int32)
+    spread = jnp.transpose(
+        neighbour_rows.reshape(blocks, group, CHUNKS, piece, features), (1, 2, 0, 3, 4)
+    ).reshape(group, CHUNKS * blocks * piece, features)
+    keys, values = exchange(
+        spread,
+        norm_gain,
+        up_weight,
+        down_weight,
+        final_gain,
+        key_weight,
+        value_weight,
+        want,
+        capacity,
+    )
+    shape = (CHUNKS, seq_count, group, capacity, piece, width)
+    return attend(
+        queries, keys.reshape(shape), values.reshape(shape), slot_index, live_counts, capacity
+    )
 
 
 def shards(
@@ -135,12 +493,12 @@
     incoming = lax.all_to_all(outgoing, "seq", split_axis=0, concat_axis=0, tiled=True)
     gathered = lax.all_gather(incoming, GROUP, axis=0, tiled=True)
     gathered = gathered.reshape(-1, features)
-    shape = (group, seq_count * capacity, part, key_weight.shape[1])
+    shape = (1, 1, group, seq_count * capacity, part, key_weight.shape[1])
     keys = jnp.dot(gathered, key_weight, preferred_element_type=jnp.float32).astype(jnp.bfloat16)
     values = jnp.dot(gathered, value_weight, preferred_element_type=jnp.float32).astype(
         jnp.bfloat16
     )
-    return attend(queries, keys.reshape(shape), values.reshape(shape), slot_index, live_counts)
+    return attend(queries, keys.reshape(shape), values.reshape(shape), slot_index, live_counts, seq_count * capacity)
 
 
 def solution(mesh):
@@ -156,6 +514,9 @@
         P("seq", None),
         P("seq"),
     )
+    members = mesh.shape["tensor"] * mesh.shape["enc"]
+    paired = mesh.shape["tensor"] == 2 and mesh.shape["enc"] == 2
+    fits = paired and NB % (members * CHUNKS * 16) == 0
     return jax.shard_map(
-        shards, mesh=mesh, in_specs=placed, out_specs=P("seq", GROUP), check_vma=False
-    )
+        exchanged_attention if fits else shards, mesh=mesh, in_specs=placed, out_specs=P("seq", GROUP), check_vma=False
+    )

time: 260 us -> 134 us (0.52)
  the two profiles are of different devices: /device:TPU:0 before, /device:TPU:28 now
where the time goes in v2:
time: 134 us
  Pallas kernels  122 us (91%)
  local copies, waits for them, and re-layouts  11.6 us (9%)
    pallas_call x1, Pallas kernels, exchange(): pl.pallas_call(functools.partial(exchange_kernel, capacity), out_shape=(o...  109 us
    pallas_call x1, Pallas kernels, attend(): pl.pallas_call(functools.partial(attend_kernel, width // DH), out_shape=j...  13.2 us
    unnamed x9, local copies, waits for them, and re-layouts  7.52 us
    reshape x1, local copies, waits for them, and re-layouts, exchanged_attention(): neighbour_rows.reshape(blocks, group, CHUNKS, piece, features)  3.22 us

profile of v2, /device:TPU:28, one launch (start us, length us, event | category | flops | bytes accessed | tf_op | source)
XLA Modules:
  0.0 133.8 jit_solution(9108542086567060910)
XLA Ops:
  0.0 0.8 copy.15
  0.8 0.1 reshape.129
  0.9 0.2 convert_reduce_fusion
  1.1 0.1 select_reduce_fusion
  1.2 0.1 broadcast_in_dim.28
  1.3 0.1 broadcast_in_dim.29
  1.3 0.6 pad.4.want_ref
  2.0 3.2 %copy.16 = bf16[8,4,2,16,1024]{4,3,0,2,1:T(8,128)(2,1)} copy(bf16[8,4,2,16,1024]{4,3,2,1,0:T(8,128)(2,1)} %bitcast.12) | data formatting | bytes 4194304 | tf_op jit(solution)/shard_map/reshape | solution.py:419
  5.2 0.0 copy-start.2
  5.2 0.0 copy-start.3
  5.2 108.6 %shard_map.100 = (bf16[16,256,1024]{2,1,0:T(8,128)(2,1)}, bf16[16,256,1024]{2,1,0:T(8,128)(2,1)}) custom-call(bf16[4,256,1024]{2,1,0:T(8,128)(2,1)} %bitcast.13, f32[1,1024]{1,0:T(1,128)} %bitcast.14, bf16[1024,1024]{1,0:T(8,128)(2,1)} %up_ref.1, bf16[1024,1024]{1,0:T(8,128)(2,1)} %down_ref.1, f32[1,1024]{1,0:T(1,128)} %bitcast.15, ...), custom_call_target="tpu_custom_call" | custom-call | flops 17179869184 | bytes 33554432 | tf_op jit(solution)/shard_map/pallas_call | solution.py:343
  113.8 0.0 copy-done.2
  113.8 0.0 copy-done.3
  113.8 0.0 copy-start
  113.8 3.4 %copy-done = bf16[16,256,1024]{2,1,0:T(8,128)(2,1)S(1)} copy-done((bf16[16,256,1024]{2,1,0:T(8,128)(2,1)S(1)}, bf16[16,256,1024]{2,1,0:T(8,128)(2,1)}, u32[]{:S(2)}) %copy-start) | copy-done | bytes 8388632
  117.2 0.0 copy-start.1
  117.2 3.4 %copy-done.1 = bf16[16,256,1024]{2,1,0:T(8,128)(2,1)S(1)} copy-done((bf16[16,256,1024]{2,1,0:T(8,128)(2,1)S(1)}, bf16[16,256,1024]{2,1,0:T(8,128)(2,1)}, u32[]{:S(2)}) %copy-start.1) | copy-done | bytes 8388632
  120.6 13.2 %shard_map.101 = bf16[1024,1024]{1,0:T(8,128)(2,1)} custom-call(s32[32]{0:T(128)S(1)} %multiply_add_fusion.slots, s32[16]{0:T(128)S(1)} %copy-done.3, bf16[1024,1024]{1,0:T(8,128)(2,1)S(1)} %copy-done.2, bf16[2,8,4,4,16,1024]{5,4,3,2,1,0:T(8,128)(2,1)S(1)} %bitcast.8, bf16[2,8,4,4,16,1024]{5,4,3,2,1,0:T(8,128)(2,1)S(1)} %bitcast.9, ...), custom_call_target="tpu_custom_call" | custom-call | tf_op jit(solution)/shard_map/pallas_call | solution.py:71
  (2 shorter events, 0.0 us)
Async XLA Ops:
  5.2 108.6 %copy-start.2 = (bf16[1024,1024]{1,0:T(8,128)(2,1)S(1)}, bf16[1024,1024]{1,0:T(8,128)(2,1)}, u32[]{:S(2)}) copy-start(bf16[1024,1024]{1,0:T(8,128)(2,1)} %q_ref.1) | copy-start | bytes 6291460
  5.2 108.6 %copy-start.3 = (s32[16]{0:T(128)S(1)}, s32[16]{0:T(128)}, u32[]{:S(2)}) copy-start(s32[16]{0:T(128)} %live.1) | copy-start | bytes 196
  113.8 3.4 %copy-start = (bf16[16,256,1024]{2,1,0:T(8,128)(2,1)S(1)}, bf16[16,256,1024]{2,1,0:T(8,128)(2,1)}, u32[]{:S(2)}) copy-start(bf16[16,256,1024]{2,1,0:T(8,128)(2,1)} %get-tuple-element.7) | copy-start | bytes 25165828
  117.2 3.4 %copy-start.1 = (bf16[16,256,1024]{2,1,0:T(8,128)(2,1)S(1)}, bf16[16,256,1024]{2,1,0:T(8,128)(2,1)}, u32[]{:S(2)}) copy-start(bf16[16,256,1024]{2,1,0:T(8,128)(2,1)} %get-tuple-element.8) | copy-start | bytes 25165828

commit v3 on v2

--- a/solution.py
+++ b/solution.py
@@ -77,13 +77,15 @@
             in_specs=[rows_of, block(0), block(1), block(0), block(1)],
             out_specs=rows_of,
         ),
-        compiler_params=pltpu.CompilerParams(vmem_limit_bytes=32 * 2**20),
+        compiler_params=pltpu.CompilerParams(vmem_limit_bytes=60 * 2**20),
     )(slots, live, queries, keys, keys, values, values)
 
 
 MESH = pl.DeviceIdType.MESH
 TILE = 256
 CHUNKS = 2
+STRIDE = 3
+AHEAD = 3
 
 
 def exchange_kernel(
@@ -102,6 +104,7 @@
     hidden,
     sums,
     core_sums,
+    far_out,
     far_sums,
     finals,
     wanted,
@@ -164,9 +167,14 @@
     for k in range(1, seq_count):
         list_copy(k).start()
 
+    def rows_of(member, c):
+        rows = rows_ref[:, member, c].reshape(chunk_rows, features)
+        return rows.astype(jnp.float32)
+
     def feed_forward(order, member):
-        rows = rows_ref[member].astype(jnp.float32)
-        normed[...] = rms_scale(rows, gain_ref[...]).astype(jnp.bfloat16)
+        for c in range(CHUNKS):
+            span = pl.ds(c * chunk_rows, chunk_rows)
+            normed[span, :] = rms_scale(rows_of(member, c), gain_ref[...]).astype(jnp.bfloat16)
 
         @pl.loop(0, up_ref.shape[1] // TILE)
         def _(n):
@@ -188,9 +196,8 @@
         )
 
     def far_copy(c):
-        span = pl.ds(c * chunk_rows, chunk_rows)
         return remote(
-            sums.at[1, span], far_sums.at[c], far_send.at[c], far_recv.at[c], x_mate
+            far_out.at[c], far_sums.at[c], far_send.at[c], far_recv.at[c], x_mate
         )
 
     feed_forward(0, 2 * (1 - ten) + 1 - enc)
@@ -199,16 +206,19 @@
     sum_copy(0).wait_recv()
     for c in range(CHUNKS):
         span = pl.ds(c * chunk_rows, chunk_rows)
-        sums[1, span, :] += core_sums[0, span, :]
+        far_out[c] = (sums[1, span, :] + core_sums[0, span, :]).astype(jnp.bfloat16)
         far_copy(c).start()
     feed_forward(2, 2 * ten + 1 - enc)
     sum_copy(1).start()
     feed_forward(3, 2 * ten + enc)
     sum_copy(1).wait_recv()
 
-    def pick_copy(s, k):
+    def offset_of(s):
+        return lax.rem(STRIDE * lax.rem(s, seq_count), seq_count)
+
+    def pick_copy(s):
         return remote(
-            outgoing.at[s], landed.at[0, s], pick_send.at[s], pick_recv.at[s], peer(k)
+            outgoing.at[s], landed.at[0, s], pick_send.at[s], pick_recv.at[s], peer(offset_of(s))
         )
 
     lane = lax.broadcasted_iota(jnp.int32, (piece, chunk_rows), 1)
@@ -227,21 +237,30 @@
             jnp.concatenate(marks, axis=0), finals[c], preferred_element_type=jnp.float32
         ).astype(jnp.bfloat16)
 
-    for c in range(CHUNKS):
+    def finish(c):
         span = pl.ds(c * chunk_rows, chunk_rows)
         far_copy(c).wait_recv()
-        encoded = rows_ref[2 * ten + enc, span, :].astype(jnp.float32) + (
-            (sums[3, span, :] + core_sums[1, span, :]) + far_sums[c]
+        encoded = rows_of(2 * ten + enc, c) + (
+            (sums[3, span, :] + core_sums[1, span, :]) + far_sums[c].astype(jnp.float32)
         )
         finals[c] = rms_scale(encoded, final_ref[...]).astype(jnp.bfloat16)
         landed[0, c * seq_count] = pick(c, want_ref[0])
 
-        @pl.loop(1, seq_count)
-        def _(k):
-            if c == 0:
-                list_copy(k).wait_recv()
-            outgoing[c * seq_count + k] = pick(c, wanted[k])
-            pick_copy(c * seq_count + k, k).start()
+    def send(s):
+        k = offset_of(s)
+
+        @pl.when(s < seq_count)
+        def _():
+            list_copy(k).wait_recv()
+
+        outgoing[s] = pick(lax.div(s, seq_count), wanted[k])
+        pick_copy(s).start()
+
+    finish(0)
+
+    @pl.loop(1, AHEAD)
+    def _(s):
+        send(s)
 
     def x_copy(s):
         return remote(landed.at[0, s], landed.at[1, s], x_send.at[s], x_recv.at[s], x_mate)
@@ -267,14 +286,22 @@
     def _(s):
         @pl.when(s < steps)
         def _():
-            k = lax.rem(s, seq_count)
-
-            @pl.when(k > 0)
+            @pl.when(lax.rem(s, seq_count) > 0)
             def _():
-                pick_copy(s, k).wait_recv()
+                pick_copy(s).wait_recv()
 
             x_copy(s).start()
             core_copy(s).start()
+            later = s + AHEAD
+            for c in range(1, CHUNKS):
+
+                @pl.when(later == c * seq_count)
+                def _():
+                    finish(c)
+
+            @pl.when(jnp.logical_and(later < steps, lax.rem(later, seq_count) > 0))
+            def _():
+                send(later)
 
         @pl.when(jnp.logical_and(s >= 1, s < steps + 1))
         def _():
@@ -322,7 +349,7 @@
     def _(s):
         @pl.when(lax.rem(s, seq_count) > 0)
         def _():
-            pick_copy(s, lax.rem(s, seq_count)).wait_send()
+            pick_copy(s).wait_send()
 
         x_copy(s).wait_send()
         core_copy(s).wait_send()
@@ -330,7 +357,8 @@
 
 
 def exchange(rows, norm_gain, up, down, final_gain, key_weight, value_weight, want, capacity):
-    group, part_rows, features = rows.shape
+    blocks, group, _, piece, features = rows.shape
+    part_rows = blocks * CHUNKS * piece
     seq_count = want.shape[0]
     steps = CHUNKS * seq_count
     width = key_weight.shape[1]
@@ -350,8 +378,7 @@
             pltpu.VMEM((part_rows, up.shape[1]), bf16),
             pltpu.VMEM((group, part_rows, features), f32),
             pltpu.VMEM((2, part_rows, features), f32),
-            pltpu.VMEM((CHUNKS, chunk_rows, features), f32),
-            pltpu.VMEM((CHUNKS, chunk_rows, features), bf16),
+            *[pltpu.VMEM((CHUNKS, chunk_rows, features), bf16) for _ in range(3)],
             pltpu.VMEM(want.shape, jnp.int32),
             pltpu.VMEM((steps, piece_rows, features), bf16),
             pltpu.VMEM((group, steps, piece_rows, features), bf16),
@@ -407,17 +434,18 @@
     width = key_weight.shape[1]
     flat_lists = block_lists.reshape(need_count)
     behind = lax.rem(lax.axis_index("seq") - flat_lists // blocks + seq_count, seq_count)
-    slot_index = behind * capacity + need_ranks(behind)
+    rank = need_ranks(behind)
+    step = lax.rem(behind * pow(STRIDE, -1, seq_count), seq_count)
+    slot_index = step * capacity + rank
+    want_index = behind * capacity + rank
     places = jnp.arange(seq_count * capacity)
-    chosen = slot_index[None, :] == places[:, None]
+    chosen = want_index[None, :] == places[:, None]
     picked = jnp.sum(jnp.where(chosen, (flat_lists % blocks)[None, :], 0), axis=1)
     want = jnp.broadcast_to(
         picked.reshape(seq_count, capacity, 1), (seq_count, capacity, blocks * piece)
     )
     want = jnp.pad(want, ((0, 0), (0, -capacity % 8), (0, 0))).astype(jnp.int32)
-    spread = jnp.transpose(
-        neighbour_rows.reshape(blocks, group, CHUNKS, piece, features), (1, 2, 0, 3, 4)
-    ).reshape(group, CHUNKS * blocks * piece, features)
+    spread = neighbour_rows.reshape(blocks, group, CHUNKS, piece, features)
     keys, values = exchange(
         spread,
         norm_gain,
@@ -516,7 +544,8 @@
     )
     members = mesh.shape["tensor"] * mesh.shape["enc"]
     paired = mesh.shape["tensor"] == 2 and mesh.shape["enc"] == 2
-    fits = paired and NB % (members * CHUNKS * 16) == 0
+    stepped = mesh.shape["seq"] > AHEAD and mesh.shape["seq"] % STRIDE != 0
+    fits = paired and stepped and NB % (members * CHUNKS * 16) == 0
     return jax.shard_map(
         exchanged_attention if fits else shards, mesh=mesh, in_specs=placed, out_specs=P("seq", GROUP), check_vma=False
     )

time: 134 us -> 113 us (0.84)
  the two profiles are of different devices: /device:TPU:28 before, /device:TPU:0 now
where the time goes in v3:
time: 113 us
  Pallas kernels  110 us (97%)
  local copies, waits for them, and re-layouts  1.63 us (1%)
    pallas_call x1, Pallas kernels, exchange(): pl.pallas_call(functools.partial(exchange_kernel, capacity), out_shape=(o...  92.5 us
    pallas_call x1, Pallas kernels, attend(): pl.pallas_call(functools.partial(attend_kernel, width // DH), out_shape=j...  17.5 us

profile of v3, /device:TPU:0, one launch (start us, length us, event | category | flops | bytes accessed | tf_op | source)
XLA Modules:
  0.0 112.5 jit_solution(17167232101364603449)
XLA Ops:
  0.0 0.8 copy.13
  0.8 0.1 reshape.126
  0.9 0.2 convert_reduce_fusion
  1.0 0.5 multiply_add_fusion
  1.6 0.1 select_reduce_fusion
  1.7 0.1 broadcast_in_dim.28
  1.8 0.1 broadcast_in_dim.29
  1.8 0.6 pad.4.want_ref
  2.5 92.5 %shard_map.100 = (bf16[16,256,1024]{2,1,0:T(8,128)(2,1)}, bf16[16,256,1024]{2,1,0:T(8,128)(2,1)}) custom-call(bf16[8,4,2,16,1024]{4,3,2,1,0:T(8,128)(2,1)} %bitcast.9, f32[1,1024]{1,0:T(1,128)} %bitcast.10, bf16[1024,1024]{1,0:T(8,128)(2,1)} %up_ref.1, bf16[1024,1024]{1,0:T(8,128)(2,1)} %down_ref.1, f32[1,1024]{1,0:T(1,128)} %bitcast.11, ...), custom_call_target="tpu_custom_call" | custom-call | flops 17179869184 | bytes 33554432 | tf_op jit(solution)/shard_map/pallas_call | solution.py:371
  95.0 17.5 %shard_map.101 = bf16[1024,1024]{1,0:T(8,128)(2,1)} custom-call(s32[32]{0:T(128)} %get-tuple-element.10.slots, s32[16]{0:T(128)} %live.1, bf16[1024,1024]{1,0:T(8,128)(2,1)} %q_ref.1, bf16[2,8,4,4,16,1024]{5,4,3,2,1,0:T(8,128)(2,1)} %bitcast.5, bf16[2,8,4,4,16,1024]{5,4,3,2,1,0:T(8,128)(2,1)} %bitcast.6, bf16[2,8,4,4,16,1024]{5,4,3,2,1,0:T(8,128)(2,1)} %bitcast.7, ...), custom_call_target="tpu_custom_call" | custom-call | tf_op jit(solution)/shard_map/pallas_call | solution.py:71
  (1 shorter events, 0.0 us)

commit v4 on v3

--- a/solution.py
+++ b/solution.py
@@ -82,7 +82,7 @@
 
 
 MESH = pl.DeviceIdType.MESH
-TILE = 256
+TILE = 1024
 CHUNKS = 2
 STRIDE = 3
 AHEAD = 3

time: 113 us -> 108 us (0.956)
  Pallas kernels: 110 us -> 105 us
    pallas_call x1, Pallas kernels: 92.5 us -> 87.2 us  [exchange(): pl.pallas_call(functools.partial(exchange_kernel, capacity), out_shape=(o...]
where the time goes in v4:
time: 108 us; the launch traced here: 107 us
  Pallas kernels  105 us (97%)
  local copies, waits for them, and re-layouts  1.63 us (2%)
    pallas_call x1, Pallas kernels, exchange(): pl.pallas_call(functools.partial(exchange_kernel, capacity), out_shape=(o...  87.2 us
    pallas_call x1, Pallas kernels, attend(): pl.pallas_call(functools.partial(attend_kernel, width // DH), out_shape=j...  17.5 us

profile of v4, /device:TPU:0, one launch (start us, length us, event | category | flops | bytes accessed | tf_op | source)
XLA Modules:
  0.0 107.2 jit_solution(17592195934183514876)
XLA Ops:
  0.0 0.8 copy.13
  0.8 0.1 reshape.126
  0.9 0.2 convert_reduce_fusion
  1.0 0.5 multiply_add_fusion
  1.6 0.1 select_reduce_fusion
  1.7 0.1 broadcast_in_dim.28
  1.8 0.1 broadcast_in_dim.29
  1.8 0.6 pad.4.want_ref
  2.5 87.2 %shard_map.100 = (bf16[16,256,1024]{2,1,0:T(8,128)(2,1)}, bf16[16,256,1024]{2,1,0:T(8,128)(2,1)}) custom-call(bf16[8,4,2,16,1024]{4,3,2,1,0:T(8,128)(2,1)} %bitcast.9, f32[1,1024]{1,0:T(1,128)} %bitcast.10, bf16[1024,1024]{1,0:T(8,128)(2,1)} %up_ref.1, bf16[1024,1024]{1,0:T(8,128)(2,1)} %down_ref.1, f32[1,1024]{1,0:T(1,128)} %bitcast.11, ...), custom_call_target="tpu_custom_call" | custom-call | flops 17179869184 | bytes 33554432 | tf_op jit(solution)/shard_map/pallas_call | solution.py:371
  89.7 17.5 %shard_map.101 = bf16[1024,1024]{1,0:T(8,128)(2,1)} custom-call(s32[32]{0:T(128)} %get-tuple-element.10.slots, s32[16]{0:T(128)} %live.1, bf16[1024,1024]{1,0:T(8,128)(2,1)} %q_ref.1, bf16[2,8,4,4,16,1024]{5,4,3,2,1,0:T(8,128)(2,1)} %bitcast.5, bf16[2,8,4,4,16,1024]{5,4,3,2,1,0:T(8,128)(2,1)} %bitcast.6, bf16[2,8,4,4,16,1024]{5,4,3,2,1,0:T(8,128)(2,1)} %bitcast.7, ...), custom_call_target="tpu_custom_call" | custom-call | tf_op jit(solution)/shard_map/pallas_call | solution.py:71
  (1 shorter events, 0.0 us)
